TPU v7x, 32 devices: a whole 2x2x4 slice. The times are simulated.
32 devices in a mesh: group: 8 (over z, core), mp: 4 (over y, x).
Axes of the slice: x: 2, y: 2, z: 4, core: 2. Of those that a mesh axis runs over, the one named last changes fastest.
Arguments:
- captions: bfloat16 [2048, 4096], P('group', 'mp'), may hold values from -6 to 6
- key_weight: bfloat16 [4096, 6144], P(None, 'mp'), may hold values from -0.09375 to 0.09375
- value_weight: bfloat16 [4096, 6144], P(None, 'mp'), may hold values from -0.09375 to 0.09375
- queries: bfloat16 [4096, 6144], P('group', 'mp'), may hold values from -400 to 400
- tile_clip: int32 [512, 1], P('group'), may hold values from 0 to 7; in each aligned block of 64 rows (0 to 63, 64 to 127, ...) at most 16 rows name the same one
- tile_length: int32 [512], P('group'), may hold values from 2 to 4, as said below
Outputs:
- attended: bfloat16 [4096, 6144], P('group', 'mp')
Inputs may be any that keep to these rules, and one draw needn't show every extreme that they name: `tile_clip`: among the tiles of one index of group at most 16 name the same clip, a bound that some block reaches of them; every clip is named by some tile. `tile_length`: the first tile of each index of group is full.
All inputs are finite; a program needn't handle non-finite values.
Results may differ from a plain program's by a relative error of at most 0.011.
Values may be sent and summed in bfloat16 or wider, within the bound.
A program may use at most 128 MiB of HBM per device.

v0:
```python
import jax
import jax.numpy as jnp
from jax import lax
from jax.sharding import PartitionSpec as P

HEAD_DIM = 128


def local(captions, key_weight, value_weight, queries, tile_clip, tile_length):
    groups = lax.axis_size("group")
    tiles = tile_length.shape[0]
    tile = captions.shape[0] // tiles
    slots = max(2, 2 * tiles // groups)
    total_slots = groups * slots
    head_cols = key_weight.shape[1]
    local_heads = head_cols // HEAD_DIM
    target = tile_clip[:, 0]
    onehot = (target[:, None] == jnp.arange(groups, dtype=jnp.int32)[None, :]).astype(jnp.int32)
    ranks = jnp.sum(jnp.cumsum(onehot, axis=0) * onehot, axis=1) - 1
    slot_of = target * slots + ranks
    select = slot_of[None, :] == jnp.arange(total_slots, dtype=jnp.int32)[:, None]
    lengths_sent = jnp.sum(jnp.where(select, tile_length[None, :], 0), axis=1).astype(jnp.bfloat16)
    select_bf = select.astype(jnp.bfloat16)
    width = captions.shape[1]
    flat = captions.reshape(tiles, tile * width)
    placed = jnp.dot(select_bf, flat, preferred_element_type=jnp.float32).astype(jnp.bfloat16)
    received = lax.all_to_all(
        placed.reshape(total_slots, tile, width), "group", split_axis=0, concat_axis=0, tiled=True
    )
    got_length = lax.all_to_all(lengths_sent, "group", split_axis=0, concat_axis=0, tiled=True)
    routed = received.reshape(total_slots * tile, received.shape[2])
    piece = lax.all_gather(routed, "mp", axis=1, tiled=True)
    key_sum = jnp.dot(piece, key_weight, preferred_element_type=jnp.float32)
    value_sum = jnp.dot(piece, value_weight, preferred_element_type=jnp.float32)
    key_rows = key_sum.astype(jnp.bfloat16)
    value_rows = value_sum.astype(jnp.bfloat16)
    positions = jnp.arange(tile, dtype=jnp.int32)
    live = (positions[None, :] < got_length.astype(jnp.int32)[:, None]).reshape(-1)
    query_heads = queries.reshape(queries.shape[0], local_heads, HEAD_DIM)
    key_heads = key_rows.reshape(-1, local_heads, HEAD_DIM)
    value_heads = value_rows.reshape(-1, local_heads, HEAD_DIM)
    scale = 1.0 / HEAD_DIM**0.5
    scores = (
        jnp.einsum("qhd,khd->hqk", query_heads, key_heads, preferred_element_type=jnp.float32)
        * scale
    )
    scores = jnp.where(live[None, None, :], scores, jnp.float32(-1e30))
    top = jnp.max(scores, axis=2, keepdims=True)
    expo = jnp.where(live[None, None, :], jnp.exp(scores - top), jnp.float32(0.0))
    weights = (expo / jnp.sum(expo, axis=2, keepdims=True)).astype(jnp.bfloat16)
    output = jnp.einsum("hqk,khd->qhd", weights, value_heads, preferred_element_type=jnp.float32)
    return output.reshape(queries.shape[0], head_cols).astype(jnp.bfloat16)


def solution(mesh):
    placed = (
        P("group", "mp"),
        P(None, "mp"),
        P(None, "mp"),
        P("group", "mp"),
        P("group", None),
        P("group"),
    )
    return jax.shard_map(
        local, mesh=mesh, in_specs=placed, out_specs=P("group", "mp"), check_vma=False
    )
```

profile of v0, /device:TPU:0, one launch (start us, length us, event | category | flops | bytes accessed | tf_op | source)
XLA Modules:
  0.0 148.9 jit_solution(14945792196000674739)
XLA Ops:
  6.5 0.0 all-gather.2.cloned.1.call-start
  6.5 0.7 fusion.13
  7.3 0.1 reduce_window_sum.11
  7.4 0.8 select_reduce_fusion.1
  8.2 0.7 add_add_fusion
  8.9 1.4 reshape.66
  10.2 0.0 copy-start.2
  10.2 0.5 convolution_convert_fusion
  10.8 0.8 reshape.67
  11.6 32.7 %all_to_all.11 = bf16[128,4,1024]{2,1,0:T(4,128)(2,1)S(1)} all-to-all(bf16[128,4,1024]{2,1,0:T(4,128)(2,1)S(1)} %reshape.67), channel_id=1, replica_groups=mesh['group'=8,'mp'=4] {'group'}, dimensions={0} | all-to-all | bytes 2097152 | tf_op jit(solution)/shard_map/all_to_all | solution.py:27
  44.3 1.1 reshape.68
  45.4 0.0 all-gather.2.cloned.1.call-update
  45.4 0.0 copy-done.2
  45.4 0.1 select_reduce_fusion
  45.5 0.7 convert_element_type.61
  46.2 3.3 %all-to-all-start.1 = ((bf16[8,16,1]{1,2,0:T(2,128)(2,1)}), bf16[8,16,1]{1,2,0:T(2,128)(2,1)S(1)}, u32[]{:S(2)}, u32[]{:S(2)}) async-start(bf16[8,16,1]{1,2,0:T(2,128)(2,1)} %convert_element_type.61), calls=%async_computation.1 | async-start | bytes 8192 | tf_op jit(solution)/shard_map/all_to_all | solution.py:30
  49.6 0.0 copy-done
  49.6 1.6 %copy.30 = bf16[512,1536]{0,1:T(8,128)(2,1)} copy(bf16[512,1536]{1,0:T(8,128)(2,1)S(1)} %copy-done) | data formatting | bytes 3145728 | tf_op args[3]
  51.2 3.9 %all-to-all-done.1 = bf16[8,16,1]{1,2,0:T(2,128)(2,1)S(1)} async-done(((bf16[8,16,1]{1,2,0:T(2,128)(2,1)}), bf16[8,16,1]{1,2,0:T(2,128)(2,1)S(1)}, u32[]{:S(2)}, u32[]{:S(2)}) %all-to-all-start.1) | async-done | bytes 288 | tf_op jit(solution)/shard_map/all_to_all | solution.py:30
  55.1 0.1 reshape.72
  55.2 0.1 iota_compare_fusion
  55.3 0.1 lt.23
  55.4 41.8 %all-gather.2.cloned.1.call-done = bf16[512,4096]{1,0:T(8,128)(2,1)} async-done(((bf16[512,1024]{1,0:T(8,128)(2,1)}), bf16[512,4096]{1,0:T(8,128)(2,1)}) %all-gather.2.cloned.1.call-update) | async-done | bytes 4194320 | tf_op jit(solution)/shard_map/all_gather | solution.py:32
  97.2 10.9 %convolution_convert_fusion.2 = bf16[512,1536]{1,0:T(8,128)(2,1)S(1)} fusion(bf16[512,4096]{1,0:T(8,128)(2,1)} %all-gather.2.cloned.1.call-done, bf16[4096,1536]{1,0:T(8,128)(2,1)} %param.8), kind=kOutput, calls=%fused_computation.14 | convolution fusion | flops 6443237376 | bytes 18350080 | tf_op jit(solution)/shard_map/dot_general | solution.py:34
  108.1 0.7 copy.27
  108.8 0.0 copy-start.1
  108.8 11.8 %convolution_convert_fusion.1 = bf16[512,1536]{1,0:T(8,128)(2,1)} fusion(bf16[512,4096]{1,0:T(8,128)(2,1)} %all-gather.2.cloned.1.call-done, bf16[4096,1536]{1,0:T(8,128)(2,1)} %param.7), kind=kOutput, calls=%fused_computation.13 | convolution fusion | flops 6443237376 | bytes 18350080 | tf_op jit(solution)/shard_map/dot_general | solution.py:33
  120.6 2.6 %copy.29 = bf16[512,1536]{0,1:T(8,128)(2,1)} copy(bf16[512,1536]{1,0:T(8,128)(2,1)} %convolution_convert_fusion.1) | data formatting | bytes 3145728 | tf_op jit(solution)/shard_map/convert_element_type | solution.py:35
  123.2 0.0 copy-done.1
  123.2 11.6 %fusion.17 = (f32[12,512]{1,0:T(8,128)S(1)}, f32[12,512,512]{1,2,0:T(8,128)}) fusion(pred[512]{0:T(512)(128)(4,1)S(1)} %lt.23, bf16[512,12,128]{0,2,1:T(8,128)(2,1)} %bitcast.33, bf16[512,12,128]{0,2,1:T(8,128)(2,1)S(1)} %bitcast.31), kind=kOutput, calls=%fused_computation.28 | convolution fusion | flops 821035520 | bytes 15753728 | tf_op jit(solution)/shard_map/sub | solution.py:49
  134.9 5.6 %fusion.10 = bf16[12,128,512]{2,1,0:T(8,128)(2,1)S(1)} fusion(bf16[512,12,128]{0,2,1:T(8,128)(2,1)S(1)} %bitcast.32, f32[12,512,512]{1,2,0:T(8,128)} %get-tuple-element.6, f32[12,512]{1,0:T(8,128)S(1)} %get-tuple-element.5), kind=kOutput, calls=%fused_computation.15 | convolution fusion | flops 812384256 | bytes 15753216 | tf_op jit(solution)/shard_map/hqk,khd->qhd/dot_general | solution.py:51
  140.4 1.6 %copy.34 = bf16[512,1536]{1,0:T(8,128)(2,1)} copy(bf16[512,1536]{0,1:T(8,128)(2,1)S(1)} %bitcast.34) | data formatting | bytes 3145728 | tf_op jit(solution)/shard_map/convert_element_type | solution.py:52
  (3 shorter events, 0.0 us)
Async XLA Ops:
  6.5 90.7 %all-gather.2.cloned.1.call-start = ((), (), s32[]{:S(2)}) async-start(), calls=%async_computation.2 | async-start | bytes 5242880 | tf_op jit(solution)/shard_map/all_gather | solution.py:32
  10.2 35.2 %copy-start.2 = (s32[64]{0:T(128)S(1)}, s32[64]{0:T(128)}, u32[]{:S(2)}) copy-start(s32[64]{0:T(128)} %param.11) | copy-start | bytes 772
  44.3 5.3 %copy-start = (bf16[512,1536]{1,0:T(8,128)(2,1)S(1)}, bf16[512,1536]{1,0:T(8,128)(2,1)}, u32[]{:S(2)}) copy-start(bf16[512,1536]{1,0:T(8,128)(2,1)} %param.9) | copy-start | bytes 4718596
  46.2 8.8 %all-to-all-start.1 = ((bf16[8,16,1]{1,2,0:T(2,128)(2,1)}), bf16[8,16,1]{1,2,0:T(2,128)(2,1)S(1)}, u32[]{:S(2)}, u32[]{:S(2)}) async-start(bf16[8,16,1]{1,2,0:T(2,128)(2,1)} %convert_element_type.61), calls=%async_computation.1 | async-start | bytes 8192 | tf_op jit(solution)/shard_map/all_to_all | solution.py:30
  108.8 14.5 %copy-start.1 = (bf16[512,1536]{0,1:T(8,128)(2,1)S(1)}, bf16[512,1536]{0,1:T(8,128)(2,1)}, u32[]{:S(2)}) copy-start(bf16[512,1536]{0,1:T(8,128)(2,1)} %copy.30) | copy-start | bytes 4718596
Sparse Core Ops, SparseCore 0:
  45.6 51.6 all-gather.1
where the time goes:
time: 149 us
  waiting for transfers between devices  45.7 us (31%)
  matrix products  40.4 us (27%)
  blocking collectives  32.7 us (22%)
  between operations  13.5 us (9%)
  local copies, waits for them, and re-layouts  10.6 us (7%)
  starting transfers between devices  3.33 us (2%)
  other arithmetic  2.54 us (2%)
    all_gather x1, waiting for transfers between devices, local(): piece = lax.all_gather(routed, 'mp', axis=1, tiled=True)  41.8 us
    all_to_all x1, blocking collectives, local(): lax.all_to_all(placed.reshape(total_slots, tile, width), 'group', split_a...  32.7 us
    dot_general x1, matrix products, local(): key_sum = jnp.dot(piece, key_weight, preferred_element_type=jnp.float32)  11.8 us
    sub x1, matrix products, local(): scores - top  11.6 us
    dot_general x1, matrix products, local(): value_sum = jnp.dot(piece, value_weight, preferred_element_type=jnp.float32)  10.9 us
    dot_general x1, matrix products, local(): jnp.einsum('hqk,khd->qhd', weights, value_heads, preferred_element_type=j...  5.58 us
    all_to_all x1, waiting for transfers between devices, local(): lax.all_to_all(lengths_sent, 'group', split_axis=0, concat_axis=0, tiled=...  3.87 us
    all_to_all x1, starting transfers between devices, local(): lax.all_to_all(lengths_sent, 'group', split_axis=0, concat_axis=0, tiled=...  3.33 us
  transfers between devices with their start and end apart: 2, of which 2 were waited for; matrix products, arithmetic and copies ran while one was open for 2% of the time, Pallas kernels for 0%

commit v1 on v0

v1 whole, which is shorter than its diff:
```python
import functools

import jax
import jax.numpy as jnp
from jax import lax
from jax.experimental import pallas as pl
from jax.experimental.pallas import tpu as pltpu
from jax.sharding import PartitionSpec as P

HEAD_DIM = 128
MESH = pl.DeviceIdType.MESH


def ring_place(i, n):
    half = n // 2
    far = i // half
    return i * (1 - far) + far * (n + half - 1 - i)


def offsets_of(groups):
    order = [0]
    for k in range(1, groups // 2 + 1):
        order.append(k)
        if groups - k != k:
            order.append(groups - k)
    return order


def widest(total, options):
    return next(o for o in options if total % o == 0)


def kernel(
    groups, n, rs, chunks, halves,
    slot_ref, cap_ref, kw_ref, vw_ref, q_hbm, out_ref,
    x, w, stage, live_stage, live, acc, q,
    w_sem, q_sem, z_send, z_recv, l_send, l_recv, r_send, r_recv,
):
    g = lax.axis_index("group")
    m = lax.axis_index("mp")
    place = ring_place(m, n)
    right = ring_place(lax.rem(place + 1, n), n)
    left = ring_place(lax.rem(place + n - 1, n), n)
    rows, width = stage.shape
    head_cols = kw_ref.shape[1]
    cols = 2 * head_cols
    hops = n // 2
    order = offsets_of(groups)

    def weight_copies(f):
        hop = (f + 1) // 2
        owner = ring_place(lax.rem(place + (n - hop if f % 2 else hop), n), n)
        part = pl.ds(pl.multiple_of(owner * width, width), width)
        return [
            pltpu.make_async_copy(kw_ref.at[part], w.at[f, :, pl.ds(0, head_cols)], w_sem.at[f, 0]),
            pltpu.make_async_copy(vw_ref.at[part], w.at[f, :, pl.ds(head_cols, head_cols)], w_sem.at[f, 1]),
        ]

    for f in range(n):
        for c in weight_copies(f):
            c.start()
    q_copy = pltpu.make_async_copy(q_hbm, q, q_sem)
    q_copy.start()

    barrier = pltpu.get_barrier_semaphore()
    for k in order[1:]:
        pl.semaphore_signal(barrier, inc=1, device_id=(lax.rem(g + k, groups), m), device_id_type=MESH)
    for side in (left, right):
        pl.semaphore_signal(barrier, inc=1, device_id=(g, side), device_id_type=MESH)

    tokens = cap_ref.shape[0]
    hit = lax.broadcasted_iota(jnp.int32, (rows, tokens), 0) == slot_ref[...]
    select = jnp.where(hit, 1.0, 0.0).astype(jnp.bfloat16)
    placed = jnp.dot(select, cap_ref[...], preferred_element_type=jnp.float32).astype(jnp.bfloat16)
    stage[...] = placed
    x[0, pl.ds(0, rs), :] = placed[:rs]
    flags = jnp.dot(
        select, jnp.ones((tokens, HEAD_DIM), jnp.bfloat16), preferred_element_type=jnp.float32
    ).astype(jnp.bfloat16)
    live_stage[...] = flags
    live[pl.ds(0, rs), :] = flags[:rs]

    pl.semaphore_wait(barrier, groups - 1 + 2)

    routes, flag_routes = [None], [None]
    for p in range(1, groups):
        part = pl.ds(p * rs, rs)
        to = (lax.rem(g + order[p], groups), m)
        routes.append(pltpu.make_async_remote_copy(
            src_ref=stage.at[part], dst_ref=x.at[0, part], send_sem=z_send.at[p],
            recv_sem=z_recv.at[p], device_id=to, device_id_type=MESH))
        flag_routes.append(pltpu.make_async_remote_copy(
            src_ref=live_stage.at[part], dst_ref=live.at[part], send_sem=l_send.at[p],
            recv_sem=l_recv.at[p], device_id=to, device_id_type=MESH))

    chunk_rows = rows // chunks
    chunk_slots = groups // chunks

    def ring_copy(c, h, side):
        first, count = c * chunk_rows, chunk_rows
        if h == hops:
            count = chunk_rows // 2
            first = first + (count if side else 0)
        part = pl.ds(first, count)
        source = 0 if h == 1 else 2 * (h - 1) - 1 + side
        target = n - 1 if h == hops else 2 * h - 1 + side
        return pltpu.make_async_remote_copy(
            src_ref=x.at[source, part], dst_ref=x.at[target, part],
            send_sem=r_send.at[c, h - 1, side], recv_sem=r_recv.at[c, h - 1, side],
            device_id=(g, left if side else right), device_id_type=MESH)

    def hop(c, h):
        if h == 1:
            for p in range(c * chunk_slots, (c + 1) * chunk_slots):
                if p:
                    routes[p].wait_recv()
        else:
            ring_copy(c, h - 1, 0).wait_recv()
            ring_copy(c, h - 1, 1).wait_recv()
        ring_copy(c, h, 0).start()
        ring_copy(c, h, 1).start()

    half_rows = rows // halves
    half_chunks = chunks // halves
    tile = widest(cols, (512, 256, 128))
    seen = set()

    def project(part, f):
        if f not in seen:
            seen.add(f)
            for c in weight_copies(f):
                c.wait()
        if f == n - 1:
            for c in range(part * half_chunks, (part + 1) * half_chunks):
                ring_copy(c, hops, 0).wait_recv()
                ring_copy(c, hops, 1).wait_recv()
        span = pl.ds(part * half_rows, half_rows)

        def body(j, carry):
            at = pl.ds(pl.multiple_of(j * tile, tile), tile)
            term = jnp.dot(x[f, span, :], w[f, :, at], preferred_element_type=jnp.float32)
            if f == 0:
                acc[span, at] = term
            else:
                acc[span, at] += term
            return carry

        lax.fori_loop(0, cols // tile, body, 0)

    for p in range(1, groups):
        if p == 1:
            ring_copy(0, 1, 0).start() if chunk_slots == 1 else None
            ring_copy(0, 1, 1).start() if chunk_slots == 1 else None
        routes[p].start()
        flag_routes[p].start()

    ready = []
    for step in range(chunks + hops - 1):
        for h in range(1, hops + 1):
            c = step - (h - 1)
            if 0 <= c < chunks and not (c == 0 and h == 1 and chunk_slots == 1):
                hop(c, h)
        for part in range(halves):
            last = (part + 1) * half_chunks - 1
            if step == last:
                ready.append((part, 0))
            for h in range(1, hops):
                if step == last + h:
                    ready.extend([(part, 2 * h - 1), (part, 2 * h)])
            if step == last + hops - 1:
                ready.append((part, n - 1))
        if ready:
            project(*ready.pop(0))
    while ready:
        project(*ready.pop(0))

    q_copy.wait()
    for p in range(1, groups):
        flag_routes[p].wait_recv()

    flags_bf = live[...]
    bias = jnp.transpose((flags_bf.astype(jnp.float32) - 1.0) * 1e30)[0:1, :]
    factor = 1.4426950408889634 / HEAD_DIM**0.5
    q_rows = q.shape[0]
    q_tile = widest(q_rows, (256, 128, 64))

    def head(i, carry):
        kcol = pl.ds(pl.multiple_of(i * HEAD_DIM, HEAD_DIM), HEAD_DIM)
        vcol = pl.ds(pl.multiple_of(head_cols + i * HEAD_DIM, HEAD_DIM), HEAD_DIM)
        keys = acc[:, kcol].astype(jnp.bfloat16)
        values = jnp.concatenate([acc[:, vcol].astype(jnp.bfloat16), live[...]], axis=1)
        for t in range(q_rows // q_tile):
            at = pl.ds(t * q_tile, q_tile)
            scores = lax.dot_general(
                q[at, kcol], keys, (((1,), (1,)), ((), ())), preferred_element_type=jnp.float32
            ) + bias
            top = jnp.max(scores, axis=1, keepdims=True)
            weights = jnp.exp2((scores - top) * factor).astype(jnp.bfloat16)
            both = jnp.dot(weights, values, preferred_element_type=jnp.float32)
            out_ref[at, kcol] = (both[:, :HEAD_DIM] / both[:, HEAD_DIM:]).astype(out_ref.dtype)
        return carry

    lax.fori_loop(0, head_cols // HEAD_DIM, head, 0)

    for p in range(1, groups):
        routes[p].wait_send()
        flag_routes[p].wait_send()
    for c in range(chunks):
        for h in range(1, hops + 1):
            for side in (0, 1):
                ring_copy(c, h, side).wait_send()


def local(captions, key_weight, value_weight, queries, tile_clip, tile_length):
    groups, n = lax.axis_size("group"), lax.axis_size("mp")
    g = lax.axis_index("group")
    tiles = tile_length.shape[0]
    tokens, width = captions.shape
    tile = tokens // tiles
    slots = max(2, 2 * tiles // groups)
    rs = -(-slots * tile // 16) * 16
    rows = groups * rs
    chunks, halves = min(groups, 8), 2
    head_cols = key_weight.shape[1]

    clip = tile_clip[:, 0]
    index = jnp.arange(tiles, dtype=jnp.int32)
    before = (clip[None, :] == clip[:, None]) & (index[None, :] < index[:, None])
    rank = jnp.sum(before.astype(jnp.int32), axis=1)
    off = lax.rem(clip - g + groups, groups)
    slot = jnp.where(off == 0, 0, jnp.where(off <= groups // 2, 2 * off - 1, 2 * (groups - off)))
    first = slot * rs + rank * tile
    token = jnp.arange(tile, dtype=jnp.int32)
    at = jnp.where(token[None, :] < tile_length[:, None], first[:, None] + token[None, :], -1)
    at = at.reshape(1, tokens)

    hops = n // 2
    bf = jnp.bfloat16
    vmem = pl.BlockSpec(memory_space=pltpu.VMEM)
    hbm = pl.BlockSpec(memory_space=pl.ANY)
    dma = pltpu.SemaphoreType.DMA
    return pl.pallas_call(
        functools.partial(kernel, groups, n, rs, chunks, halves),
        out_shape=jax.ShapeDtypeStruct(queries.shape, bf),
        in_specs=[vmem, vmem, hbm, hbm, hbm],
        out_specs=vmem,
        scratch_shapes=[
            pltpu.VMEM((n, rows, width), bf),
            pltpu.VMEM((n, width, 2 * head_cols), bf),
            pltpu.VMEM((rows, width), bf),
            pltpu.VMEM((rows, HEAD_DIM), bf),
            pltpu.VMEM((rows, HEAD_DIM), bf),
            pltpu.VMEM((rows, 2 * head_cols), jnp.float32),
            pltpu.VMEM(queries.shape, bf),
            dma((n, 2)), dma(()),
            dma((groups,)), dma((groups,)), dma((groups,)), dma((groups,)),
            dma((chunks, hops, 2)), dma((chunks, hops, 2)),
        ],
        compiler_params=pltpu.CompilerParams(
            collective_id=0, has_side_effects=True, vmem_limit_bytes=58 * 1024 * 1024
        ),
        cost_estimate=pl.CostEstimate(
            flops=4 * rows * n * width * head_cols + 4 * queries.size * rows,
            bytes_accessed=4 * key_weight.size + 4 * queries.size,
            transcendentals=queries.size * rows // HEAD_DIM,
        ),
    )(at, captions, key_weight, value_weight, queries)


def solution(mesh):
    placed = (
        P("group", "mp"),
        P(None, "mp"),
        P(None, "mp"),
        P("group", "mp"),
        P("group", None),
        P("group"),
    )
    return jax.shard_map(
        local, mesh=mesh, in_specs=placed, out_specs=P("group", "mp"), check_vma=False
    )
```

time: 149 us -> 65.4 us (0.44)
  Pallas kernels: 0 us -> 58.6 us
  waiting for transfers between devices: 45.7 us -> 0 us
  matrix products: 40.4 us -> 0 us
  blocking collectives: 32.7 us -> 0 us
  between operations: 13.5 us -> 0.02 us
  local copies, waits for them, and re-layouts: 10.6 us -> 3.32 us
  starting transfers between devices: 3.33 us -> 0 us
    pallas_call x0 -> x1, Pallas kernels: none -> 58.6 us  [local(): pl.pallas_call(functools.partial(kernel, groups, n, rs, chunks, halves),...]
    all_gather x1 -> x0, waiting for transfers between devices: 41.8 us -> none  [local(): piece = lax.all_gather(routed, 'mp', axis=1, tiled=True)]
    all_to_all x1 -> x0, blocking collectives: 32.7 us -> none  [local(): lax.all_to_all(placed.reshape(total_slots, tile, width), 'group', split_a...]
    dot_general x4 -> x0, matrix products: 28.8 us -> none  [the longest x1 11.8 us: local(): key_sum = jnp.dot(piece, key_weight, preferred_element_type=jnp.float32)]
    sub x1 -> x0, matrix products: 11.6 us -> none  [local(): scores - top]
    convert_element_type x5 -> x0, local copies, waits for them, and re-layouts: 5.65 us -> none  [the longest x1 2.61 us: local(): key_rows = key_sum.astype(jnp.bfloat16)]
    all_to_all x1 -> x0, waiting for transfers between devices: 3.87 us -> none  [local(): lax.all_to_all(lengths_sent, 'group', split_axis=0, concat_axis=0, tiled=...]
    all_to_all x1 -> x0, starting transfers between devices: 3.33 us -> none  [local(): lax.all_to_all(lengths_sent, 'group', split_axis=0, concat_axis=0, tiled=...]
  transfers between devices with their start and end apart: 2 -> 0, of which waited for: 2 -> 0; matrix products, arithmetic and copies ran while one was open for 2% -> 0% of each run, Pallas kernels for 0% -> 0%
where the time goes in v1:
time: 65.4 us; the launch traced here: 64.3 us
  Pallas kernels  58.6 us (90%)
  local copies, waits for them, and re-layouts  3.32 us (5%)
  other arithmetic  2.32 us (4%)
    pallas_call x1, Pallas kernels, local(): pl.pallas_call(functools.partial(kernel, groups, n, rs, chunks, halves),...  58.6 us
    unnamed x1, local copies, waits for them, and re-layouts  2.65 us

profile of v1, /device:TPU:0, one launch (start us, length us, event | category | flops | bytes accessed | tf_op | source)
XLA Modules:
  0.0 64.3 jit_solution(3087184317166936351)
XLA Ops:
  0.0 0.9 %convert_reduce_fusion = s32[64]{0:T(128)S(1)} fusion(s32[64]{0:T(128)} %bitcast.7), kind=kLoop, calls=%fused_computation.1 | loop fusion | flops 20416 | bytes 512 | tf_op jit(solution)/shard_map/reduce_sum | solution.py:229
  0.9 0.7 %fusion.4 = s32[64]{0:T(128)S(1)} fusion(s32[64]{0:T(128)S(1)} %convert_reduce_fusion, s32[64,1]{0,1:T(1,128)} %param.10, s32[]{:T(128)S(6)} %axis_index.15), kind=kLoop, calls=%fused_computation.12 | loop fusion | flops 1216 | bytes 772 | tf_op jit(solution)/shard_map/add | solution.py:234
  1.6 0.7 %add_select_fusion = s32[64,4]{1,0:T(8,128)S(1)} fusion(s32[64]{0:T(128)S(1)} %fusion.4, s32[64]{0:T(128)} %param.11), kind=kLoop, calls=%fused_computation | loop fusion | flops 768 | bytes 1536 | tf_op jit(solution)/shard_map/jit(_where)/select_n | solution.py:234
  2.3 0.7 %select_n.27.slot_ref = s32[1,256]{1,0:T(1,128)} reshape(s32[64,4]{1,0:T(8,128)S(1)} %add_select_fusion) | data formatting | bytes 2048 | tf_op jit(solution)/shard_map/jit(_where)/select_n | solution.py:234
  3.0 58.6 %shard_map.64 = bf16[512,1536]{1,0:T(8,128)(2,1)} custom-call(s32[1,256]{1,0:T(1,128)} %select_n.27.slot_ref, bf16[256,1024]{1,0:T(8,128)(2,1)} %cap_ref.1, bf16[4096,1536]{1,0:T(8,128)(2,1)} %kw_ref.1, bf16[4096,1536]{1,0:T(8,128)(2,1)} %vw_ref.1, bf16[512,1536]{1,0:T(8,128)(2,1)} %q_hbm.1), custom_call_target="tpu_custom_call" | custom-call | flops 14495514624 | bytes 28311552 | tf_op jit(solution)/shard_map/pallas_call | solution.py:242
  61.6 2.7 %copy.8 = bf16[512,1536]{1,0:T(8,128)(2,1)} copy(bf16[512,1536]{1,0:T(8,128)(2,1)} %shard_map.64) | data formatting | bytes 3145728

commit v2 on v1

--- a/solution.py
+++ b/solution.py
@@ -32,7 +32,7 @@
 
 def kernel(
     groups, n, rs, chunks, halves,
-    slot_ref, cap_ref, kw_ref, vw_ref, q_hbm, out_ref,
+    clip_ref, length_ref, cap_ref, kw_ref, vw_ref, q_hbm, out_ref,
     x, w, stage, live_stage, live, acc, q,
     w_sem, q_sem, z_send, z_recv, l_send, l_recv, r_send, r_recv,
 ):
@@ -68,17 +68,48 @@
     for side in (left, right):
         pl.semaphore_signal(barrier, inc=1, device_id=(g, side), device_id_type=MESH)
 
-    tokens = cap_ref.shape[0]
-    hit = lax.broadcasted_iota(jnp.int32, (rows, tokens), 0) == slot_ref[...]
+    f32, i32 = jnp.float32, jnp.int32
+    tokens, tiles = cap_ref.shape[0], length_ref.shape[1]
+    size = tokens // tiles
+    row = lax.broadcasted_iota(i32, (tiles, tiles), 0)
+    column = lax.broadcasted_iota(i32, (tiles, tiles), 1)
+    def upright(across):
+        return jnp.sum(jnp.where(row == column, across, 0.0), axis=1, keepdims=True)
+
+    clip_across = clip_ref[...].astype(f32)
+    clip = upright(clip_across)
+    length = upright(length_ref[...].astype(f32))
+    rank = jnp.sum(
+        jnp.where((clip == clip_across) & (column < row), 1.0, 0.0), axis=1, keepdims=True
+    )
+    off = clip.astype(i32) - g
+    off = jnp.where(off < 0, off + groups, off)
+    slot = jnp.where(off == 0, 0, jnp.where(off <= groups // 2, 2 * off - 1, 2 * (groups - off)))
+    first = slot.astype(f32) * rs + rank * size
+    part_of = lax.broadcasted_iota(i32, (tiles, tokens), 1) - size * lax.broadcasted_iota(
+        i32, (tiles, tokens), 0
+    )
+    token = part_of.astype(f32)
+    own = (part_of >= 0) & (part_of < size)
+    at_row = jnp.sum(
+        jnp.where(own & (token < length), first + token + 1.0, 0.0), axis=0, keepdims=True
+    ) - 1.0
+    hit = lax.broadcasted_iota(i32, (rows, tokens), 0) == at_row.astype(i32)
     select = jnp.where(hit, 1.0, 0.0).astype(jnp.bfloat16)
-    placed = jnp.dot(select, cap_ref[...], preferred_element_type=jnp.float32).astype(jnp.bfloat16)
+    placed = jnp.dot(select, cap_ref[...], preferred_element_type=f32).astype(jnp.bfloat16)
     stage[...] = placed
     x[0, pl.ds(0, rs), :] = placed[:rs]
-    flags = jnp.dot(
-        select, jnp.ones((tokens, HEAD_DIM), jnp.bfloat16), preferred_element_type=jnp.float32
-    ).astype(jnp.bfloat16)
-    live_stage[...] = flags
-    live[pl.ds(0, rs), :] = flags[:rs]
+    flags = lax.dot_general(
+        jnp.ones((16, tokens), jnp.bfloat16), select, (((1,), (1,)), ((), ())),
+        preferred_element_type=f32,
+    )
+    blank = jnp.zeros((16, 128 - rs), f32)
+    for p in range(groups):
+        flag = jnp.concatenate([flags[:, p * rs:(p + 1) * rs], blank], axis=1).astype(jnp.bfloat16)
+        if p:
+            live_stage[p] = flag
+        else:
+            live[p] = flag
 
     pl.semaphore_wait(barrier, groups - 1 + 2)
 
@@ -90,7 +121,7 @@
             src_ref=stage.at[part], dst_ref=x.at[0, part], send_sem=z_send.at[p],
             recv_sem=z_recv.at[p], device_id=to, device_id_type=MESH))
         flag_routes.append(pltpu.make_async_remote_copy(
-            src_ref=live_stage.at[part], dst_ref=live.at[part], send_sem=l_send.at[p],
+            src_ref=live_stage.at[p], dst_ref=live.at[p], send_sem=l_send.at[p],
             recv_sem=l_recv.at[p], device_id=to, device_id_type=MESH))
 
     chunk_rows = rows // chunks
@@ -131,7 +162,7 @@
             for c in weight_copies(f):
                 c.wait()
         if f == n - 1:
-            for c in range(part * half_chunks, (part + 1) * half_chunks):
+            for c in both(part):
                 ring_copy(c, hops, 0).wait_recv()
                 ring_copy(c, hops, 1).wait_recv()
         span = pl.ds(part * half_rows, half_rows)
@@ -154,53 +185,79 @@
         routes[p].start()
         flag_routes[p].start()
 
-    ready = []
-    for step in range(chunks + hops - 1):
-        for h in range(1, hops + 1):
-            c = step - (h - 1)
-            if 0 <= c < chunks and not (c == 0 and h == 1 and chunk_slots == 1):
+    def both(part):
+        return range(part * half_chunks, (part + 1) * half_chunks)
+
+    early = [[(c, 1)] for c in both(0)] + [[] for _ in range(hops - 1)]
+    for h in range(2, hops + 1):
+        for c in both(0):
+            early[c + h - 1].append((c, h))
+    events = early[:half_chunks - 1]
+    rest = early[half_chunks - 1:]
+    events.append(rest[0] + [(0, 0)])
+    for i in range(max(half_chunks, hops - 1)):
+        event = []
+        if i < half_chunks:
+            event.append((half_chunks + i, 1))
+        if i + 1 < len(rest):
+            event += rest[i + 1]
+        events.append(event + [(0, 0)])
+    for h in range(2, hops + 1):
+        events.append([(c, h) for c in both(1)])
+
+    units = [(0, f) for f in range(n)] + [(1, f) for f in range(n - 1)]
+    for event in events:
+        for c, h in event:
+            if h == 0:
+                if units:
+                    project(*units.pop(0))
+            elif not (c == 0 and h == 1 and chunk_slots == 1):
                 hop(c, h)
-        for part in range(halves):
-            last = (part + 1) * half_chunks - 1
-            if step == last:
-                ready.append((part, 0))
-            for h in range(1, hops):
-                if step == last + h:
-                    ready.extend([(part, 2 * h - 1), (part, 2 * h)])
-            if step == last + hops - 1:
-                ready.append((part, n - 1))
-        if ready:
-            project(*ready.pop(0))
-    while ready:
-        project(*ready.pop(0))
+    while units:
+        project(*units.pop(0))
 
     q_copy.wait()
     for p in range(1, groups):
         flag_routes[p].wait_recv()
-
-    flags_bf = live[...]
-    bias = jnp.transpose((flags_bf.astype(jnp.float32) - 1.0) * 1e30)[0:1, :]
+    for c in both(1):
+        ring_copy(c, hops, 0).wait_recv()
+        ring_copy(c, hops, 1).wait_recv()
+
+    flag_row = jnp.concatenate([live[p][0:1, :rs] for p in range(groups)], axis=1)
+    bias = (flag_row.astype(f32) - 1.0) * 1e30
     factor = 1.4426950408889634 / HEAD_DIM**0.5
     q_rows = q.shape[0]
     q_tile = widest(q_rows, (256, 128, 64))
 
-    def head(i, carry):
-        kcol = pl.ds(pl.multiple_of(i * HEAD_DIM, HEAD_DIM), HEAD_DIM)
-        vcol = pl.ds(pl.multiple_of(head_cols + i * HEAD_DIM, HEAD_DIM), HEAD_DIM)
-        keys = acc[:, kcol].astype(jnp.bfloat16)
-        values = jnp.concatenate([acc[:, vcol].astype(jnp.bfloat16), live[...]], axis=1)
-        for t in range(q_rows // q_tile):
-            at = pl.ds(t * q_tile, q_tile)
-            scores = lax.dot_general(
-                q[at, kcol], keys, (((1,), (1,)), ((), ())), preferred_element_type=jnp.float32
-            ) + bias
-            top = jnp.max(scores, axis=1, keepdims=True)
-            weights = jnp.exp2((scores - top) * factor).astype(jnp.bfloat16)
-            both = jnp.dot(weights, values, preferred_element_type=jnp.float32)
-            out_ref[at, kcol] = (both[:, :HEAD_DIM] / both[:, HEAD_DIM:]).astype(out_ref.dtype)
+    heads = head_cols // HEAD_DIM
+    group_heads = widest(heads, (2, 1))
+    wide = group_heads * HEAD_DIM
+    done, last = pl.ds(0, half_rows), pl.ds(half_rows, half_rows)
+    ones = jnp.ones((rows, HEAD_DIM), jnp.bfloat16)
+
+    def finished(at):
+        tail = acc[last, at] + jnp.dot(x[n - 1, last, :], w[n - 1, :, at], preferred_element_type=f32)
+        return jnp.concatenate([acc[done, at].astype(jnp.bfloat16), tail.astype(jnp.bfloat16)], axis=0)
+
+    def some_heads(i, carry):
+        keys = finished(pl.ds(pl.multiple_of(i * wide, wide), wide))
+        values = finished(pl.ds(pl.multiple_of(head_cols + i * wide, HEAD_DIM), wide))
+        for j in range(group_heads):
+            mine = slice(j * HEAD_DIM, (j + 1) * HEAD_DIM)
+            col = pl.ds(pl.multiple_of(i * wide + j * HEAD_DIM, HEAD_DIM), HEAD_DIM)
+            with_ones = jnp.concatenate([values[:, mine], ones], axis=1)
+            for t in range(q_rows // q_tile):
+                at = pl.ds(t * q_tile, q_tile)
+                scores = lax.dot_general(
+                    q[at, col], keys[:, mine], (((1,), (1,)), ((), ())), preferred_element_type=f32
+                ) + bias
+                top = jnp.max(scores, axis=1, keepdims=True)
+                weights = jnp.exp2((scores - top) * factor).astype(jnp.bfloat16)
+                total = jnp.dot(weights, with_ones, preferred_element_type=f32)
+                out_ref[at, col] = (total[:, :HEAD_DIM] / total[:, HEAD_DIM:]).astype(out_ref.dtype)
         return carry
 
-    lax.fori_loop(0, head_cols // HEAD_DIM, head, 0)
+    lax.fori_loop(0, heads // group_heads, some_heads, 0)
 
     for p in range(1, groups):
         routes[p].wait_send()
@@ -213,7 +270,6 @@
 
 def local(captions, key_weight, value_weight, queries, tile_clip, tile_length):
     groups, n = lax.axis_size("group"), lax.axis_size("mp")
-    g = lax.axis_index("group")
     tiles = tile_length.shape[0]
     tokens, width = captions.shape
     tile = tokens // tiles
@@ -223,17 +279,6 @@
     chunks, halves = min(groups, 8), 2
     head_cols = key_weight.shape[1]
 
-    clip = tile_clip[:, 0]
-    index = jnp.arange(tiles, dtype=jnp.int32)
-    before = (clip[None, :] == clip[:, None]) & (index[None, :] < index[:, None])
-    rank = jnp.sum(before.astype(jnp.int32), axis=1)
-    off = lax.rem(clip - g + groups, groups)
-    slot = jnp.where(off == 0, 0, jnp.where(off <= groups // 2, 2 * off - 1, 2 * (groups - off)))
-    first = slot * rs + rank * tile
-    token = jnp.arange(tile, dtype=jnp.int32)
-    at = jnp.where(token[None, :] < tile_length[:, None], first[:, None] + token[None, :], -1)
-    at = at.reshape(1, tokens)
-
     hops = n // 2
     bf = jnp.bfloat16
     vmem = pl.BlockSpec(memory_space=pltpu.VMEM)
@@ -242,14 +287,14 @@
     return pl.pallas_call(
         functools.partial(kernel, groups, n, rs, chunks, halves),
         out_shape=jax.ShapeDtypeStruct(queries.shape, bf),
-        in_specs=[vmem, vmem, hbm, hbm, hbm],
+        in_specs=[vmem, vmem, vmem, hbm, hbm, hbm],
         out_specs=vmem,
         scratch_shapes=[
             pltpu.VMEM((n, rows, width), bf),
             pltpu.VMEM((n, width, 2 * head_cols), bf),
             pltpu.VMEM((rows, width), bf),
-            pltpu.VMEM((rows, HEAD_DIM), bf),
-            pltpu.VMEM((rows, HEAD_DIM), bf),
+            pltpu.VMEM((groups, 16, 128), bf),
+            pltpu.VMEM((groups, 16, 128), bf),
             pltpu.VMEM((rows, 2 * head_cols), jnp.float32),
             pltpu.VMEM(queries.shape, bf),
             dma((n, 2)), dma(()),
@@ -264,7 +309,7 @@
             bytes_accessed=4 * key_weight.size + 4 * queries.size,
             transcendentals=queries.size * rows // HEAD_DIM,
         ),
-    )(at, captions, key_weight, value_weight, queries)
+    )(tile_clip.reshape(1, tiles), tile_length.reshape(1, tiles), captions, key_weight, value_weight, queries)
 
 
 def solution(mesh):

time: 65.4 us -> 56.6 us (0.87)
  the two profiles are of different devices: /device:TPU:0 before, /device:TPU:1 now
where the time goes in v2:
time: 56.6 us; the launch traced here: 56.5 us
  Pallas kernels  53.8 us (95%)
  local copies, waits for them, and re-layouts  2.65 us (5%)
    pallas_call x1, Pallas kernels, local(): pl.pallas_call(functools.partial(kernel, groups, n, rs, chunks, halves),...  53.8 us
    unnamed x1, local copies, waits for them, and re-layouts  2.65 us

profile of v2, /device:TPU:1, one launch (start us, length us, event | category | flops | bytes accessed | tf_op | source)
XLA Modules:
  0.0 56.5 jit_solution(2807419409082248065)
XLA Ops:
  0.0 53.8 %shard_map.64 = bf16[512,1536]{1,0:T(8,128)(2,1)} custom-call(s32[1,64]{1,0:T(1,128)} %bitcast.2, s32[1,64]{1,0:T(1,128)} %bitcast.3, bf16[256,1024]{1,0:T(8,128)(2,1)} %cap_ref.1, bf16[4096,1536]{1,0:T(8,128)(2,1)} %kw_ref.1, bf16[4096,1536]{1,0:T(8,128)(2,1)} %vw_ref.1, bf16[512,1536]{1,0:T(8,128)(2,1)} %q_hbm.1), custom_call_target="tpu_custom_call" | custom-call | flops 14495514624 | bytes 28311552 | tf_op jit(solution)/shard_map/pallas_call | solution.py:287
  53.8 2.7 %copy.8 = bf16[512,1536]{1,0:T(8,128)(2,1)} copy(bf16[512,1536]{1,0:T(8,128)(2,1)} %shard_map.64) | data formatting | bytes 3145728

commit v3 on v2

--- a/solution.py
+++ b/solution.py
@@ -17,13 +17,13 @@
     return i * (1 - far) + far * (n + half - 1 - i)
 
 
-def offsets_of(groups):
-    order = [0]
-    for k in range(1, groups // 2 + 1):
-        order.append(k)
-        if groups - k != k:
-            order.append(groups - k)
-    return order
+def partner(g, k):
+    bit = 1
+    while bit <= k:
+        if k & bit:
+            g = g + bit - 2 * bit * lax.rem(g // bit, 2)
+        bit *= 2
+    return g
 
 
 def widest(total, options):
@@ -45,7 +45,6 @@
     head_cols = kw_ref.shape[1]
     cols = 2 * head_cols
     hops = n // 2
-    order = offsets_of(groups)
 
     def weight_copies(f):
         hop = (f + 1) // 2
@@ -63,8 +62,8 @@
     q_copy.start()
 
     barrier = pltpu.get_barrier_semaphore()
-    for k in order[1:]:
-        pl.semaphore_signal(barrier, inc=1, device_id=(lax.rem(g + k, groups), m), device_id_type=MESH)
+    for k in range(1, groups):
+        pl.semaphore_signal(barrier, inc=1, device_id=(partner(g, k), m), device_id_type=MESH)
     for side in (left, right):
         pl.semaphore_signal(barrier, inc=1, device_id=(g, side), device_id_type=MESH)
 
@@ -82,9 +81,7 @@
     rank = jnp.sum(
         jnp.where((clip == clip_across) & (column < row), 1.0, 0.0), axis=1, keepdims=True
     )
-    off = clip.astype(i32) - g
-    off = jnp.where(off < 0, off + groups, off)
-    slot = jnp.where(off == 0, 0, jnp.where(off <= groups // 2, 2 * off - 1, 2 * (groups - off)))
+    slot = jnp.bitwise_xor(clip.astype(i32), jnp.full(clip.shape, g, i32))
     first = slot.astype(f32) * rs + rank * size
     part_of = lax.broadcasted_iota(i32, (tiles, tokens), 1) - size * lax.broadcasted_iota(
         i32, (tiles, tokens), 0
@@ -116,7 +113,7 @@
     routes, flag_routes = [None], [None]
     for p in range(1, groups):
         part = pl.ds(p * rs, rs)
-        to = (lax.rem(g + order[p], groups), m)
+        to = (partner(g, p), m)
         routes.append(pltpu.make_async_remote_copy(
             src_ref=stage.at[part], dst_ref=x.at[0, part], send_sem=z_send.at[p],
             recv_sem=z_recv.at[p], device_id=to, device_id_type=MESH))
@@ -156,12 +153,14 @@
     tile = widest(cols, (512, 256, 128))
     seen = set()
 
-    def project(part, f):
+    pieces = 2 if cols // tile > 1 else 1
+
+    def project(part, f, piece):
         if f not in seen:
             seen.add(f)
             for c in weight_copies(f):
                 c.wait()
-        if f == n - 1:
+        if f == n - 1 and piece == 0:
             for c in both(part):
                 ring_copy(c, hops, 0).wait_recv()
                 ring_copy(c, hops, 1).wait_recv()
@@ -176,43 +175,36 @@
                 acc[span, at] += term
             return carry
 
-        lax.fori_loop(0, cols // tile, body, 0)
-
+        steps = cols // tile
+        lax.fori_loop(steps * piece // pieces, steps * (piece + 1) // pieces, body, 0)
+
+    if chunk_slots == 1:
+        hop(0, 1)
     for p in range(1, groups):
-        if p == 1:
-            ring_copy(0, 1, 0).start() if chunk_slots == 1 else None
-            ring_copy(0, 1, 1).start() if chunk_slots == 1 else None
         routes[p].start()
         flag_routes[p].start()
 
     def both(part):
         return range(part * half_chunks, (part + 1) * half_chunks)
 
-    early = [[(c, 1)] for c in both(0)] + [[] for _ in range(hops - 1)]
-    for h in range(2, hops + 1):
-        for c in both(0):
-            early[c + h - 1].append((c, h))
-    events = early[:half_chunks - 1]
-    rest = early[half_chunks - 1:]
-    events.append(rest[0] + [(0, 0)])
-    for i in range(max(half_chunks, hops - 1)):
-        event = []
-        if i < half_chunks:
-            event.append((half_chunks + i, 1))
-        if i + 1 < len(rest):
-            event += rest[i + 1]
-        events.append(event + [(0, 0)])
-    for h in range(2, hops + 1):
-        events.append([(c, h) for c in both(1)])
-
-    units = [(0, f) for f in range(n)] + [(1, f) for f in range(n - 1)]
-    for event in events:
-        for c, h in event:
-            if h == 0:
-                if units:
-                    project(*units.pop(0))
-            elif not (c == 0 and h == 1 and chunk_slots == 1):
-                hop(c, h)
+    events = sorted(
+        ((c, h) for c in range(chunks) for h in range(1, hops + 1)),
+        key=lambda e: (e[0] + (1.5 if e[0] < half_chunks else 2.5) * (e[1] - 1), e[1]),
+    )
+    units = [(0, f, i) for f in range(n) for i in range(pieces)]
+    units += [(1, f, i) for f in range(n - 1) for i in range(pieces)]
+    begun = set()
+
+    def ready(part, f, piece):
+        need = hops if f == n - 1 else (f + 1) // 2 + 1
+        return all((c, need) in begun for c in both(part))
+
+    for c, h in events:
+        if not (c == 0 and h == 1 and chunk_slots == 1):
+            hop(c, h)
+        begun.add((c, h))
+        if units and ready(*units[0]):
+            project(*units.pop(0))
     while units:
         project(*units.pop(0))
 

time: 56.6 us -> 61.3 us (1.083)
  the two profiles are of different devices: /device:TPU:1 before, /device:TPU:0 now
where the time goes in v3:
time: 61.3 us; the launch traced here: 61.1 us
  Pallas kernels  58.5 us (95%)
  local copies, waits for them, and re-layouts  2.65 us (4%)
    pallas_call x1, Pallas kernels, local(): pl.pallas_call(functools.partial(kernel, groups, n, rs, chunks, halves),...  58.5 us
    unnamed x1, local copies, waits for them, and re-layouts  2.65 us

profile of v3, /device:TPU:0, one launch (start us, length us, event | category | flops | bytes accessed | tf_op | source)
XLA Modules:
  0.0 61.1 jit_solution(2577800948257137379)
XLA Ops:
  0.0 58.5 %shard_map.64 = bf16[512,1536]{1,0:T(8,128)(2,1)} custom-call(s32[1,64]{1,0:T(1,128)} %bitcast.2, s32[1,64]{1,0:T(1,128)} %bitcast.3, bf16[256,1024]{1,0:T(8,128)(2,1)} %cap_ref.1, bf16[4096,1536]{1,0:T(8,128)(2,1)} %kw_ref.1, bf16[4096,1536]{1,0:T(8,128)(2,1)} %vw_ref.1, bf16[512,1536]{1,0:T(8,128)(2,1)} %q_hbm.1), custom_call_target="tpu_custom_call" | custom-call | flops 14495514624 | bytes 28311552 | tf_op jit(solution)/shard_map/pallas_call | solution.py:279
  58.5 2.7 %copy.8 = bf16[512,1536]{1,0:T(8,128)(2,1)} copy(bf16[512,1536]{1,0:T(8,128)(2,1)} %shard_map.64) | data formatting | bytes 3145728

commit v4 on v3

--- a/solution.py
+++ b/solution.py
@@ -24,6 +24,16 @@
             g = g + bit - 2 * bit * lax.rem(g // bit, 2)
         bit *= 2
     return g
+
+
+def offsets_of(groups):
+    half = groups // 2
+    near, far = list(range(1, half)), list(range(half, groups))
+    order = [0]
+    while near or far:
+        order += near[:1] + far[:1]
+        near, far = near[1:], far[1:]
+    return order
 
 
 def widest(total, options):
@@ -45,6 +55,7 @@
     head_cols = kw_ref.shape[1]
     cols = 2 * head_cols
     hops = n // 2
+    order = offsets_of(groups)
 
     def weight_copies(f):
         hop = (f + 1) // 2
@@ -81,7 +92,9 @@
     rank = jnp.sum(
         jnp.where((clip == clip_across) & (column < row), 1.0, 0.0), axis=1, keepdims=True
     )
-    slot = jnp.bitwise_xor(clip.astype(i32), jnp.full(clip.shape, g, i32))
+    off = jnp.bitwise_xor(clip.astype(i32), jnp.full(clip.shape, g, i32))
+    far = jnp.minimum(2 * off + 2 - groups, groups - 1)
+    slot = jnp.where(off == 0, 0, jnp.where(off < groups // 2, 2 * off - 1, far))
     first = slot.astype(f32) * rs + rank * size
     part_of = lax.broadcasted_iota(i32, (tiles, tokens), 1) - size * lax.broadcasted_iota(
         i32, (tiles, tokens), 0
@@ -113,7 +126,7 @@
     routes, flag_routes = [None], [None]
     for p in range(1, groups):
         part = pl.ds(p * rs, rs)
-        to = (partner(g, p), m)
+        to = (partner(g, order[p]), m)
         routes.append(pltpu.make_async_remote_copy(
             src_ref=stage.at[part], dst_ref=x.at[0, part], send_sem=z_send.at[p],
             recv_sem=z_recv.at[p], device_id=to, device_id_type=MESH))

time: 61.3 us -> 59.3 us (0.967)
  Pallas kernels: 58.5 us -> 56.5 us
    pallas_call x1, Pallas kernels: 58.5 us -> 56.5 us  [local(): pl.pallas_call(functools.partial(kernel, groups, n, rs, chunks, halves),...]
where the time goes in v4:
time: 59.3 us; the launch traced here: 59.1 us
  Pallas kernels  56.5 us (95%)
  local copies, waits for them, and re-layouts  2.65 us (4%)
    pallas_call x1, Pallas kernels, local(): pl.pallas_call(functools.partial(kernel, groups, n, rs, chunks, halves),...  56.5 us
    unnamed x1, local copies, waits for them, and re-layouts  2.65 us

profile of v4, /device:TPU:0, one launch (start us, length us, event | category | flops | bytes accessed | tf_op | source)
XLA Modules:
  0.0 59.1 jit_solution(3605365296860489821)
XLA Ops:
  0.0 56.5 %shard_map.64 = bf16[512,1536]{1,0:T(8,128)(2,1)} custom-call(s32[1,64]{1,0:T(1,128)} %bitcast.2, s32[1,64]{1,0:T(1,128)} %bitcast.3, bf16[256,1024]{1,0:T(8,128)(2,1)} %cap_ref.1, bf16[4096,1536]{1,0:T(8,128)(2,1)} %kw_ref.1, bf16[4096,1536]{1,0:T(8,128)(2,1)} %vw_ref.1, bf16[512,1536]{1,0:T(8,128)(2,1)} %q_hbm.1), custom_call_target="tpu_custom_call" | custom-call | flops 14495514624 | bytes 28311552 | tf_op jit(solution)/shard_map/pallas_call | solution.py:292
  56.5 2.7 %copy.8 = bf16[512,1536]{1,0:T(8,128)(2,1)} copy(bf16[512,1536]{1,0:T(8,128)(2,1)} %shard_map.64) | data formatting | bytes 3145728

commit v5 on v4

--- a/solution.py
+++ b/solution.py
@@ -43,7 +43,7 @@
 def kernel(
     groups, n, rs, chunks, halves,
     clip_ref, length_ref, cap_ref, kw_ref, vw_ref, q_hbm, out_ref,
-    x, w, stage, live_stage, live, acc, q,
+    x, w, stage, live_stage, live, acc, q, early_sum, early_top,
     w_sem, q_sem, z_send, z_recv, l_send, l_recv, r_send, r_recv,
 ):
     g = lax.axis_index("group")
@@ -200,69 +200,123 @@
     def both(part):
         return range(part * half_chunks, (part + 1) * half_chunks)
 
-    events = sorted(
-        ((c, h) for c in range(chunks) for h in range(1, hops + 1)),
-        key=lambda e: (e[0] + (1.5 if e[0] < half_chunks else 2.5) * (e[1] - 1), e[1]),
-    )
-    units = [(0, f, i) for f in range(n) for i in range(pieces)]
-    units += [(1, f, i) for f in range(n - 1) for i in range(pieces)]
-    begun = set()
-
-    def ready(part, f, piece):
-        need = hops if f == n - 1 else (f + 1) // 2 + 1
-        return all((c, need) in begun for c in both(part))
-
-    for c, h in events:
-        if not (c == 0 and h == 1 and chunk_slots == 1):
-            hop(c, h)
-        begun.add((c, h))
-        if units and ready(*units[0]):
-            project(*units.pop(0))
-    while units:
-        project(*units.pop(0))
-
-    q_copy.wait()
-    for p in range(1, groups):
-        flag_routes[p].wait_recv()
-    for c in both(1):
-        ring_copy(c, hops, 0).wait_recv()
-        ring_copy(c, hops, 1).wait_recv()
-
-    flag_row = jnp.concatenate([live[p][0:1, :rs] for p in range(groups)], axis=1)
-    bias = (flag_row.astype(f32) - 1.0) * 1e30
     factor = 1.4426950408889634 / HEAD_DIM**0.5
     q_rows = q.shape[0]
     q_tile = widest(q_rows, (256, 128, 64))
-
     heads = head_cols // HEAD_DIM
     group_heads = widest(heads, (2, 1))
     wide = group_heads * HEAD_DIM
-    done, last = pl.ds(0, half_rows), pl.ds(half_rows, half_rows)
-    ones = jnp.ones((rows, HEAD_DIM), jnp.bfloat16)
-
-    def finished(at):
-        tail = acc[last, at] + jnp.dot(x[n - 1, last, :], w[n - 1, :, at], preferred_element_type=f32)
-        return jnp.concatenate([acc[done, at].astype(jnp.bfloat16), tail.astype(jnp.bfloat16)], axis=0)
-
-    def some_heads(i, carry):
-        keys = finished(pl.ds(pl.multiple_of(i * wide, wide), wide))
-        values = finished(pl.ds(pl.multiple_of(head_cols + i * wide, HEAD_DIM), wide))
+    halves_of = pl.ds(0, half_rows), pl.ds(half_rows, half_rows)
+    ones = jnp.ones((half_rows, HEAD_DIM), jnp.bfloat16)
+    part_slots = groups // halves
+
+    def bias_of(part):
+        slots_of = range(part * part_slots, (part + 1) * part_slots)
+        row = jnp.concatenate([live[p][0:1, :rs] for p in slots_of], axis=1)
+        return (row.astype(f32) - 1.0) * 1e30
+
+    def columns_of(i):
+        return (pl.ds(pl.multiple_of(i * wide, HEAD_DIM), wide),
+                pl.ds(pl.multiple_of(head_cols + i * wide, HEAD_DIM), wide))
+
+    def each_head(i, keys, values, use):
         for j in range(group_heads):
             mine = slice(j * HEAD_DIM, (j + 1) * HEAD_DIM)
             col = pl.ds(pl.multiple_of(i * wide + j * HEAD_DIM, HEAD_DIM), HEAD_DIM)
+            double = pl.ds(pl.multiple_of(2 * i * wide + 2 * j * HEAD_DIM, HEAD_DIM), 2 * HEAD_DIM)
             with_ones = jnp.concatenate([values[:, mine], ones], axis=1)
             for t in range(q_rows // q_tile):
                 at = pl.ds(t * q_tile, q_tile)
                 scores = lax.dot_general(
                     q[at, col], keys[:, mine], (((1,), (1,)), ((), ())), preferred_element_type=f32
-                ) + bias
-                top = jnp.max(scores, axis=1, keepdims=True)
-                weights = jnp.exp2((scores - top) * factor).astype(jnp.bfloat16)
-                total = jnp.dot(weights, with_ones, preferred_element_type=f32)
-                out_ref[at, col] = (total[:, :HEAD_DIM] / total[:, HEAD_DIM:]).astype(out_ref.dtype)
-        return carry
-
-    lax.fori_loop(0, heads // group_heads, some_heads, 0)
+                )
+                use(scores, with_ones, at, col, double)
+
+    def weigh(scores, top, with_ones):
+        weights = jnp.exp2((scores - top) * factor).astype(jnp.bfloat16)
+        return jnp.dot(weights, with_ones, preferred_element_type=f32)
+
+    def attend_early(begin, end):
+        if begin == 0:
+            q_copy.wait()
+            for p in range(1, part_slots):
+                flag_routes[p].wait_recv()
+        bias = bias_of(0)
+
+        def use(scores, with_ones, at, col, double):
+            scores = scores + bias
+            top = jnp.max(scores, axis=1, keepdims=True)
+            early_top[at, col] = jnp.broadcast_to(top, (q_tile, HEAD_DIM))
+            early_sum[at, double] = weigh(scores, top, with_ones)
+
+        def body(i, carry):
+            keys, values = (acc[halves_of[0], c].astype(jnp.bfloat16) for c in columns_of(i))
+            each_head(i, keys, values, use)
+            return carry
+
+        lax.fori_loop(begin, end, body, 0)
+
+    def attend_late():
+        bias = bias_of(1)
+
+        def use(scores, with_ones, at, col, double):
+            scores = scores + bias
+            before = early_top[at, col]
+            top = jnp.maximum(jnp.max(scores, axis=1, keepdims=True), before)
+            total = weigh(scores, top[:, :1], with_ones)
+            keep = jnp.exp2((before - top) * factor)
+            earlier = early_sum[at, double]
+            above = total[:, :HEAD_DIM] + keep * earlier[:, :HEAD_DIM]
+            below = total[:, HEAD_DIM:] + keep * earlier[:, HEAD_DIM:]
+            out_ref[at, col] = (above / below).astype(out_ref.dtype)
+
+        def body(i, carry):
+            keys, values = (
+                (acc[halves_of[1], c] + jnp.dot(
+                    x[n - 1, halves_of[1], :], w[n - 1, :, c], preferred_element_type=f32
+                )).astype(jnp.bfloat16)
+                for c in columns_of(i)
+            )
+            each_head(i, keys, values, use)
+            return carry
+
+        lax.fori_loop(0, heads // group_heads, body, 0)
+
+    events = sorted(
+        ((c, h) for c in range(chunks) for h in range(1, hops + 1)),
+        key=lambda e: (e[0] + (1.5 if e[0] < half_chunks else half_chunks + 0.5) * (e[1] - 1), e[1]),
+    )
+    units = [(0, f, i) for f in range(n) for i in range(pieces)]
+    units += [(1, f, i) for f in range(n - 1) for i in range(pieces)]
+    begun = set()
+
+    def ready(part, f, piece):
+        need = hops if f == n - 1 else (f + 1) // 2 + 1
+        return all((c, need) in begun for c in both(part))
+
+    loops = heads // group_heads
+    for c, h in events:
+        if (c, h) == (chunks - 1, hops):
+            while units and units[0][0] == 0:
+                project(*units.pop(0))
+            attend_early(0, loops // 2)
+        if not (c == 0 and h == 1 and chunk_slots == 1):
+            hop(c, h)
+        begun.add((c, h))
+        later = c >= half_chunks
+        for _ in range(1 if not later or c == half_chunks else 2):
+            if units and not (later and h > 1) and ready(*units[0]):
+                project(*units.pop(0))
+    attend_early(loops // 2, loops)
+    while units:
+        project(*units.pop(0))
+
+    for p in range(part_slots, groups):
+        flag_routes[p].wait_recv()
+    for c in both(1):
+        ring_copy(c, hops, 0).wait_recv()
+        ring_copy(c, hops, 1).wait_recv()
+    attend_late()
 
     for p in range(1, groups):
         routes[p].wait_send()
@@ -302,6 +356,8 @@
             pltpu.VMEM((groups, 16, 128), bf),
             pltpu.VMEM((rows, 2 * head_cols), jnp.float32),
             pltpu.VMEM(queries.shape, bf),
+            pltpu.VMEM((queries.shape[0], 2 * head_cols), jnp.float32),
+            pltpu.VMEM(queries.shape, jnp.float32),
             dma((n, 2)), dma(()),
             dma((groups,)), dma((groups,)), dma((groups,)), dma((groups,)),
             dma((chunks, hops, 2)), dma((chunks, hops, 2)),

time: 59.3 us -> 61.9 us (1.044)
  Pallas kernels: 56.5 us -> 59.1 us
    pallas_call x1, Pallas kernels: 56.5 us -> 59.1 us  [local(): pl.pallas_call(functools.partial(kernel, groups, n, rs, chunks, halves),...]
where the time goes in v5:
time: 61.9 us; the launch traced here: 61.7 us
  Pallas kernels  59.1 us (95%)
  local copies, waits for them, and re-layouts  2.65 us (4%)
    pallas_call x1, Pallas kernels, local(): pl.pallas_call(functools.partial(kernel, groups, n, rs, chunks, halves),...  59.1 us
    unnamed x1, local copies, waits for them, and re-layouts  2.65 us

profile of v5, /device:TPU:0, one launch (start us, length us, event | category | flops | bytes accessed | tf_op | source)
XLA Modules:
  0.0 61.7 jit_solution(1884405186027584609)
XLA Ops:
  0.0 59.1 %shard_map.64 = bf16[512,1536]{1,0:T(8,128)(2,1)} custom-call(s32[1,64]{1,0:T(1,128)} %bitcast.2, s32[1,64]{1,0:T(1,128)} %bitcast.3, bf16[256,1024]{1,0:T(8,128)(2,1)} %cap_ref.1, bf16[4096,1536]{1,0:T(8,128)(2,1)} %kw_ref.1, bf16[4096,1536]{1,0:T(8,128)(2,1)} %vw_ref.1, bf16[512,1536]{1,0:T(8,128)(2,1)} %q_hbm.1), custom_call_target="tpu_custom_call" | custom-call | flops 14495514624 | bytes 28311552 | tf_op jit(solution)/shard_map/pallas_call | solution.py:346
  59.1 2.7 %copy.8 = bf16[512,1536]{1,0:T(8,128)(2,1)} copy(bf16[512,1536]{1,0:T(8,128)(2,1)} %shard_map.64) | data formatting | bytes 3145728

commit v6 on v2

--- a/solution.py
+++ b/solution.py
@@ -52,8 +52,8 @@
         owner = ring_place(lax.rem(place + (n - hop if f % 2 else hop), n), n)
         part = pl.ds(pl.multiple_of(owner * width, width), width)
         return [
-            pltpu.make_async_copy(kw_ref.at[part], w.at[f, :, pl.ds(0, head_cols)], w_sem.at[f, 0]),
-            pltpu.make_async_copy(vw_ref.at[part], w.at[f, :, pl.ds(head_cols, head_cols)], w_sem.at[f, 1]),
+            pltpu.make_async_copy(kw_ref.at[part], w.at[pl.ds(f * width, width), pl.ds(0, head_cols)], w_sem.at[f, 0]),
+            pltpu.make_async_copy(vw_ref.at[part], w.at[pl.ds(f * width, width), pl.ds(head_cols, head_cols)], w_sem.at[f, 1]),
         ]
 
     for f in range(n):
@@ -98,7 +98,7 @@
     select = jnp.where(hit, 1.0, 0.0).astype(jnp.bfloat16)
     placed = jnp.dot(select, cap_ref[...], preferred_element_type=f32).astype(jnp.bfloat16)
     stage[...] = placed
-    x[0, pl.ds(0, rs), :] = placed[:rs]
+    x[pl.ds(0, rs), pl.ds(0, width)] = placed[:rs]
     flags = lax.dot_general(
         jnp.ones((16, tokens), jnp.bfloat16), select, (((1,), (1,)), ((), ())),
         preferred_element_type=f32,
@@ -118,7 +118,7 @@
         part = pl.ds(p * rs, rs)
         to = (lax.rem(g + order[p], groups), m)
         routes.append(pltpu.make_async_remote_copy(
-            src_ref=stage.at[part], dst_ref=x.at[0, part], send_sem=z_send.at[p],
+            src_ref=stage.at[part], dst_ref=x.at[part, pl.ds(0, width)], send_sem=z_send.at[p],
             recv_sem=z_recv.at[p], device_id=to, device_id_type=MESH))
         flag_routes.append(pltpu.make_async_remote_copy(
             src_ref=live_stage.at[p], dst_ref=live.at[p], send_sem=l_send.at[p],
@@ -136,7 +136,8 @@
         source = 0 if h == 1 else 2 * (h - 1) - 1 + side
         target = n - 1 if h == hops else 2 * h - 1 + side
         return pltpu.make_async_remote_copy(
-            src_ref=x.at[source, part], dst_ref=x.at[target, part],
+            src_ref=x.at[part, pl.ds(source * width, width)],
+            dst_ref=x.at[part, pl.ds(target * width, width)],
             send_sem=r_send.at[c, h - 1, side], recv_sem=r_recv.at[c, h - 1, side],
             device_id=(g, left if side else right), device_id_type=MESH)
 
@@ -153,23 +154,25 @@
 
     half_rows = rows // halves
     half_chunks = chunks // halves
-    tile = widest(cols, (512, 256, 128))
+    tile = widest(cols, (1536, 768, 256, 128))
     seen = set()
 
-    def project(part, f):
-        if f not in seen:
-            seen.add(f)
-            for c in weight_copies(f):
-                c.wait()
-        if f == n - 1:
+    def project(part, f, count):
+        for block in range(f, f + count):
+            if block not in seen:
+                seen.add(block)
+                for c in weight_copies(block):
+                    c.wait()
+        if f + count == n:
             for c in both(part):
                 ring_copy(c, hops, 0).wait_recv()
                 ring_copy(c, hops, 1).wait_recv()
+        depth = pl.ds(f * width, count * width)
         span = pl.ds(part * half_rows, half_rows)
 
         def body(j, carry):
             at = pl.ds(pl.multiple_of(j * tile, tile), tile)
-            term = jnp.dot(x[f, span, :], w[f, :, at], preferred_element_type=jnp.float32)
+            term = jnp.dot(x[span, depth], w[depth, at], preferred_element_type=jnp.float32)
             if f == 0:
                 acc[span, at] = term
             else:
@@ -201,18 +204,29 @@
             event.append((half_chunks + i, 1))
         if i + 1 < len(rest):
             event += rest[i + 1]
-        events.append(event + [(0, 0)])
+        events.append(event + [(0, 0)] if i else event)
     for h in range(2, hops + 1):
         events.append([(c, h) for c in both(1)])
 
-    units = [(0, f) for f in range(n)] + [(1, f) for f in range(n - 1)]
+    pairs = [(f, 2) for f in range(1, n - 1, 2)]
+    units = [(0, 0, 1)] + [(0, *pair) for pair in pairs] + [(0, n - 1, 1), (1, 0, 1)]
+    units += [(1, *pair) for pair in pairs]
+    begun = set()
+
+    def ready(part, f, count):
+        last = f + count - 1
+        need = hops if last == n - 1 else (last + 1) // 2 + 1
+        return all((c, need) in begun for c in both(part))
+
     for event in events:
         for c, h in event:
             if h == 0:
-                if units:
+                if units and ready(*units[0]):
                     project(*units.pop(0))
-            elif not (c == 0 and h == 1 and chunk_slots == 1):
+                continue
+            if not (c == 0 and h == 1 and chunk_slots == 1):
                 hop(c, h)
+            begun.add((c, h))
     while units:
         project(*units.pop(0))
 
@@ -227,7 +241,7 @@
     bias = (flag_row.astype(f32) - 1.0) * 1e30
     factor = 1.4426950408889634 / HEAD_DIM**0.5
     q_rows = q.shape[0]
-    q_tile = widest(q_rows, (256, 128, 64))
+    q_tile = widest(q_rows, (512, 256, 128, 64))
 
     heads = head_cols // HEAD_DIM
     group_heads = widest(heads, (2, 1))
@@ -236,7 +250,10 @@
     ones = jnp.ones((rows, HEAD_DIM), jnp.bfloat16)
 
     def finished(at):
-        tail = acc[last, at] + jnp.dot(x[n - 1, last, :], w[n - 1, :, at], preferred_element_type=f32)
+        tail = acc[last, at] + jnp.dot(
+            x[last, pl.ds((n - 1) * width, width)], w[pl.ds((n - 1) * width, width), at],
+            preferred_element_type=f32,
+        )
         return jnp.concatenate([acc[done, at].astype(jnp.bfloat16), tail.astype(jnp.bfloat16)], axis=0)
 
     def some_heads(i, carry):
@@ -290,8 +307,8 @@
         in_specs=[vmem, vmem, vmem, hbm, hbm, hbm],
         out_specs=vmem,
         scratch_shapes=[
-            pltpu.VMEM((n, rows, width), bf),
-            pltpu.VMEM((n, width, 2 * head_cols), bf),
+            pltpu.VMEM((rows, n * width), bf),
+            pltpu.VMEM((n * width, 2 * head_cols), bf),
             pltpu.VMEM((rows, width), bf),
             pltpu.VMEM((groups, 16, 128), bf),
             pltpu.VMEM((groups, 16, 128), bf),
@@ -302,7 +319,7 @@
             dma((chunks, hops, 2)), dma((chunks, hops, 2)),
         ],
         compiler_params=pltpu.CompilerParams(
-            collective_id=0, has_side_effects=True, vmem_limit_bytes=58 * 1024 * 1024
+            collective_id=0, has_side_effects=True, vmem_limit_bytes=50 * 1024 * 1024
         ),
         cost_estimate=pl.CostEstimate(
             flops=4 * rows * n * width * head_cols + 4 * queries.size * rows,

time: 56.6 us -> 56.4 us (level)
  the two profiles are of different devices: /device:TPU:1 before, /device:TPU:0 now
where the time goes in v6:
time: 56.4 us; the launch traced here: 55.9 us
  Pallas kernels  50.9 us (90%)
  local copies, waits for them, and re-layouts  4.9 us (9%)
    pallas_call x1, Pallas kernels, local(): pl.pallas_call(functools.partial(kernel, groups, n, rs, chunks, halves),...  50.9 us
    unnamed x9, local copies, waits for them, and re-layouts  4.9 us

profile of v6, /device:TPU:0, one launch (start us, length us, event | category | flops | bytes accessed | tf_op | source)
XLA Modules:
  0.0 55.9 jit_solution(17655016504480718673)
XLA Ops:
  0.0 0.0 copy-start
  0.0 1.4 %copy-done = bf16[512,1536]{1,0:T(8,128)(2,1)S(1)} copy-done((bf16[512,1536]{1,0:T(8,128)(2,1)S(1)}, bf16[512,1536]{1,0:T(8,128)(2,1)}, u32[]{:S(2)}) %copy-start) | copy-done | bytes 1572888
  1.4 0.0 copy-start.1
  1.4 1.0 %copy-done.1 = bf16[256,1024]{1,0:T(8,128)(2,1)S(1)} copy-done((bf16[256,1024]{1,0:T(8,128)(2,1)S(1)}, bf16[256,1024]{1,0:T(8,128)(2,1)}, u32[]{:S(2)}) %copy-start.1) | copy-done | bytes 524312
  2.5 0.0 copy-start.2
  2.5 0.7 %copy-done.2 = s32[64,1]{0,1:T(1,128)S(1)} copy-done((s32[64,1]{0,1:T(1,128)S(1)}, s32[64,1]{0,1:T(1,128)}, u32[]{:S(2)}) %copy-start.2) | copy-done | bytes 280
  3.1 0.0 copy-start.3
  3.1 0.7 %copy-done.3 = s32[64]{0:T(128)S(1)} copy-done((s32[64]{0:T(128)S(1)}, s32[64]{0:T(128)}, u32[]{:S(2)}) %copy-start.3) | copy-done | bytes 280
  3.8 50.9 %shard_map.64 = bf16[512,1536]{1,0:T(8,128)(2,1)S(1)} custom-call(s32[1,64]{1,0:T(1,128)S(1)} %bitcast.2, s32[1,64]{1,0:T(1,128)S(1)} %bitcast.3, bf16[256,1024]{1,0:T(8,128)(2,1)S(1)} %copy-done.1, bf16[4096,1536]{1,0:T(8,128)(2,1)} %kw_ref.1, bf16[4096,1536]{1,0:T(8,128)(2,1)} %vw_ref.1, bf16[512,1536]{1,0:T(8,128)(2,1)S(1)} %copy-done), custom_call_target="tpu_custom_call" | custom-call | flops 14495514624 | bytes 28311552 | tf_op jit(solution)/shard_map/pallas_call | solution.py:304
  54.7 1.1 %copy.8 = bf16[512,1536]{1,0:T(8,128)(2,1)} copy(bf16[512,1536]{1,0:T(8,128)(2,1)S(1)} %shard_map.64) | data formatting | bytes 3145728
Async XLA Ops:
  0.0 1.4 %copy-start = (bf16[512,1536]{1,0:T(8,128)(2,1)S(1)}, bf16[512,1536]{1,0:T(8,128)(2,1)}, u32[]{:S(2)}) copy-start(bf16[512,1536]{1,0:T(8,128)(2,1)} %q_hbm.1) | copy-start | bytes 4718596
  1.4 1.0 %copy-start.1 = (bf16[256,1024]{1,0:T(8,128)(2,1)S(1)}, bf16[256,1024]{1,0:T(8,128)(2,1)}, u32[]{:S(2)}) copy-start(bf16[256,1024]{1,0:T(8,128)(2,1)} %cap_ref.1) | copy-start | bytes 1572868
  2.5 0.7 %copy-start.2 = (s32[64,1]{0,1:T(1,128)S(1)}, s32[64,1]{0,1:T(1,128)}, u32[]{:S(2)}) copy-start(s32[64,1]{0,1:T(1,128)} %param.10) | copy-start | bytes 772
  3.1 0.7 %copy-start.3 = (s32[64]{0:T(128)S(1)}, s32[64]{0:T(128)}, u32[]{:S(2)}) copy-start(s32[64]{0:T(128)} %param.11) | copy-start | bytes 772

commit v7 on v6

--- a/solution.py
+++ b/solution.py
@@ -32,9 +32,9 @@
 
 def kernel(
     groups, n, rs, chunks, halves,
-    clip_ref, length_ref, cap_ref, kw_ref, vw_ref, q_hbm, out_ref,
+    clip_hbm, length_hbm, cap_hbm, kw_ref, vw_ref, q_hbm, out_ref,
     x, w, stage, live_stage, live, acc, q,
-    w_sem, q_sem, z_send, z_recv, l_send, l_recv, r_send, r_recv,
+    clip_ref, length_ref, cap_ref, in_sem, w_sem, q_sem, z_send, z_recv, l_send, l_recv, r_send, r_recv,
 ):
     g = lax.axis_index("group")
     m = lax.axis_index("mp")
@@ -47,6 +47,14 @@
     hops = n // 2
     order = offsets_of(groups)
 
+    inputs = [
+        pltpu.make_async_copy(clip_hbm, clip_ref, in_sem.at[0]),
+        pltpu.make_async_copy(length_hbm, length_ref, in_sem.at[1]),
+        pltpu.make_async_copy(cap_hbm, cap_ref, in_sem.at[2]),
+    ]
+    for c in inputs:
+        c.start()
+
     def weight_copies(f):
         hop = (f + 1) // 2
         owner = ring_place(lax.rem(place + (n - hop if f % 2 else hop), n), n)
@@ -68,6 +76,8 @@
     for side in (left, right):
         pl.semaphore_signal(barrier, inc=1, device_id=(g, side), device_id_type=MESH)
 
+    for c in inputs:
+        c.wait()
     f32, i32 = jnp.float32, jnp.int32
     tokens, tiles = cap_ref.shape[0], length_ref.shape[1]
     size = tokens // tiles
@@ -299,12 +309,12 @@
     hops = n // 2
     bf = jnp.bfloat16
     vmem = pl.BlockSpec(memory_space=pltpu.VMEM)
-    hbm = pl.BlockSpec(memory_space=pl.ANY)
+    hbm = pl.BlockSpec(memory_space=pltpu.HBM)
     dma = pltpu.SemaphoreType.DMA
     return pl.pallas_call(
         functools.partial(kernel, groups, n, rs, chunks, halves),
         out_shape=jax.ShapeDtypeStruct(queries.shape, bf),
-        in_specs=[vmem, vmem, vmem, hbm, hbm, hbm],
+        in_specs=[hbm] * 6,
         out_specs=vmem,
         scratch_shapes=[
             pltpu.VMEM((rows, n * width), bf),
@@ -314,12 +324,15 @@
             pltpu.VMEM((groups, 16, 128), bf),
             pltpu.VMEM((rows, 2 * head_cols), jnp.float32),
             pltpu.VMEM(queries.shape, bf),
-            dma((n, 2)), dma(()),
+            pltpu.VMEM((1, tiles), jnp.int32),
+            pltpu.VMEM((1, tiles), jnp.int32),
+            pltpu.VMEM(captions.shape, bf),
+            dma((3,)), dma((n, 2)), dma(()),
             dma((groups,)), dma((groups,)), dma((groups,)), dma((groups,)),
             dma((chunks, hops, 2)), dma((chunks, hops, 2)),
         ],
         compiler_params=pltpu.CompilerParams(
-            collective_id=0, has_side_effects=True, vmem_limit_bytes=50 * 1024 * 1024
+            collective_id=0, has_side_effects=True, vmem_limit_bytes=58 * 1024 * 1024
         ),
         cost_estimate=pl.CostEstimate(
             flops=4 * rows * n * width * head_cols + 4 * queries.size * rows,

time: 56.4 us -> 60.1 us (1.066)
  Pallas kernels: 50.9 us -> 57.3 us
  local copies, waits for them, and re-layouts: 4.9 us -> 2.65 us
    pallas_call x1, Pallas kernels: 50.9 us -> 57.3 us  [local(): pl.pallas_call(functools.partial(kernel, groups, n, rs, chunks, halves),...]
    unnamed x9 -> x1, local copies, waits for them, and re-layouts: 4.9 us -> 2.65 us
where the time goes in v7:
time: 60.1 us; the launch traced here: 60 us
  Pallas kernels  57.3 us (95%)
  local copies, waits for them, and re-layouts  2.65 us (4%)
    pallas_call x1, Pallas kernels, local(): pl.pallas_call(functools.partial(kernel, groups, n, rs, chunks, halves),...  57.3 us
    unnamed x1, local copies, waits for them, and re-layouts  2.65 us

profile of v7, /device:TPU:0, one launch (start us, length us, event | category | flops | bytes accessed | tf_op | source)
XLA Modules:
  0.0 60.0 jit_solution(2288915476655430446)
XLA Ops:
  0.0 57.3 %shard_map.64 = bf16[512,1536]{1,0:T(8,128)(2,1)} custom-call(s32[1,64]{1,0:T(1,128)} %bitcast.2, s32[1,64]{1,0:T(1,128)} %bitcast.3, bf16[256,1024]{1,0:T(8,128)(2,1)} %cap_hbm.1, bf16[4096,1536]{1,0:T(8,128)(2,1)} %kw_ref.1, bf16[4096,1536]{1,0:T(8,128)(2,1)} %vw_ref.1, bf16[512,1536]{1,0:T(8,128)(2,1)} %q_hbm.1), custom_call_target="tpu_custom_call" | custom-call | flops 14495514624 | bytes 28311552 | tf_op jit(solution)/shard_map/pallas_call | solution.py:314
  57.3 2.7 %copy.8 = bf16[512,1536]{1,0:T(8,128)(2,1)} copy(bf16[512,1536]{1,0:T(8,128)(2,1)} %shard_map.64) | data formatting | bytes 3145728
